TPU v7x, 256 devices: a whole 4x4x8 slice. The times are simulated.
256 devices in a mesh: seq: 16 (over y, z_lo, core), row: 4 (over z_hi), col: 4 (over x).
Axes of the slice: x: 4, y: 4, z: 8 (z_hi: 4, z_lo: 2; z = z_hi * 2 + z_lo), core: 2. Of those that a mesh axis runs over, the one named last changes fastest.
Arguments:
- tokens: bfloat16 [8192, 4096], P(('seq', 'row'), 'col'), may hold values from -6 to 6
- w_uvqk: bfloat16 [4096, 8192], P(('seq', 'row'), 'col'), may hold values from -0.09375 to 0.09375
- w_out: bfloat16 [2048, 4096], P('col', ('seq', 'row')), may hold values from -0.375 to 0.375
- rab_table: float32 [16, 32], replicated, may hold values from -4 to 4
- norm_gain: float32 [16, 128], replicated, may hold values from 0.5 to 2
- user_lengths: int32 [4], replicated, may hold values from 1 to 6144, 8192 in all
- bucket_ids: int32 [8192], P('seq'), may hold values from 0 to 8191, as said below
Outputs:
- layer_out: bfloat16 [8192, 4096], P(('seq', 'row'), 'col')
Inputs may be any that keep to these rules, and one draw needn't show every extreme that they name: bucket_ids never fall from one token to the next.
All inputs are finite; a program needn't handle non-finite values.
Results may differ from a plain program's by a relative error of at most 0.014.
Values may be sent and summed in bfloat16 or wider, within the bound.
No kernel may reach another device: no remote copies, remote signals or barrier semaphores. Data moves between devices by JAX's collectives and lax.ppermute only.
A program may use at most 64 MiB of HBM per device.

v0:
```python
import math
import jax
import jax.numpy as jnp
from jax import lax
from jax.sharding import PartitionSpec as P

DH = 128
NB = 32
norm_eps = 1e-05


def user_index(user_ends, positions):
    return jnp.sum((user_ends[None, :] <= positions[:, None]).astype(jnp.int32), axis=1)


def bucket_biases(table_rows, bucket_gap):
    one_hot = (bucket_gap[:, :, None] == jnp.arange(NB, dtype=jnp.int32)[None, None, :]).astype(
        jnp.float32
    )
    return jnp.einsum(
        "qkb,hb->hqk",
        one_hot,
        table_rows,
        precision=lax.Precision.HIGHEST,
        preferred_element_type=jnp.float32,
    )


def on_device(tokens, w_uvqk, w_out, rab_table, norm_gain, user_lengths, bucket_ids):
    feature_rows = lax.all_gather(tokens, "col", axis=1, tiled=True)
    local_rows = tokens.shape[0]
    width_cols = w_uvqk.shape[1]
    row_index = lax.axis_index("row")
    col_index = lax.axis_index("col")
    seq_index = lax.axis_index("seq")
    projected = jnp.dot(
        feature_rows,
        lax.all_gather(w_uvqk, ("seq", "row"), axis=0, tiled=True),
        preferred_element_type=jnp.float32,
    )
    local_heads = width_cols // (4 * DH)
    activated = jax.nn.silu(projected).astype(jnp.bfloat16).reshape(local_rows, local_heads, 4, DH)
    head_major = lax.all_to_all(activated, "row", split_axis=1, concat_axis=0, tiled=True)
    block_len = head_major.shape[0]
    per_device = head_major.shape[1]
    user_ends = jnp.cumsum(user_lengths)
    query_pos = seq_index * block_len + jnp.arange(block_len, dtype=jnp.int32)
    query_user = user_index(user_ends, query_pos)
    first_head = col_index * local_heads + row_index * per_device
    rab_rows = lax.dynamic_slice_in_dim(rab_table, first_head, per_device, 0)
    gain_rows = lax.dynamic_slice_in_dim(norm_gain, first_head, per_device, 0)
    queries = head_major[:, :, 2]
    key_value = head_major[:, :, 1:4:2]
    score_scale = DH ** (-0.5)
    running = jnp.zeros((block_len, per_device, DH), jnp.float32)
    kv_piece = lax.all_gather(key_value, "seq", axis=0, tiled=True)
    key_bucket = lax.all_gather(bucket_ids, "seq", axis=0, tiled=True)
    key_count = kv_piece.shape[0]
    sub_size = math.gcd(key_count, 256)
    sub_count = key_count // sub_size

    def sub_block(accum_in, sub_index):
        sub_first = sub_index * sub_size
        kv_sub = lax.dynamic_slice_in_dim(kv_piece, sub_first, sub_size, 0)
        bucket_sub = lax.dynamic_slice_in_dim(key_bucket, sub_first, sub_size, 0)
        key_pos = sub_first + jnp.arange(sub_size, dtype=jnp.int32)
        key_user = user_index(user_ends, key_pos)
        visible = (query_user[:, None] == key_user[None, :]) & (
            key_pos[None, :] <= query_pos[:, None]
        )
        bucket_gap = jnp.clip(bucket_ids[:, None] - bucket_sub[None, :], 0, NB - 1)
        biases = bucket_biases(rab_rows, bucket_gap)
        scores = (
            jnp.dot(queries[:, 0], kv_sub[:, 0, 1].T, preferred_element_type=jnp.float32)
            * score_scale
        )
        scores = scores + biases[0]
        weights = jnp.where(visible, jax.nn.silu(scores), jnp.float32(0.0)).astype(jnp.bfloat16)
        per_head = [jnp.dot(weights, kv_sub[:, 0, 0], preferred_element_type=jnp.float32)]
        accum_out = accum_in + jnp.stack(per_head, axis=1)
        return (accum_out, None)

    running, _ = lax.scan(sub_block, running, jnp.arange(sub_count, dtype=jnp.int32))
    head_mean = jnp.mean(running, axis=-1, keepdims=True)
    centered = running - head_mean
    head_var = jnp.mean(centered * centered, axis=-1, keepdims=True)
    normed = centered * lax.rsqrt(head_var + norm_eps) * gain_rows[None, :, :]
    gated = (normed * head_major[:, :, 0].astype(jnp.float32)).astype(jnp.bfloat16)
    token_major = lax.all_to_all(gated, "row", split_axis=0, concat_axis=1, tiled=True)
    gated_rows = token_major.reshape(local_rows, local_heads * DH)
    partials = jnp.dot(
        gated_rows,
        lax.all_gather(w_out, ("seq", "row"), axis=1, tiled=True),
        preferred_element_type=jnp.float32,
    )
    summed = lax.psum_scatter(
        partials.astype(jnp.bfloat16), "col", scatter_dimension=1, tiled=True
    ).astype(jnp.float32)
    return (tokens.astype(jnp.float32) + summed).astype(jnp.bfloat16)


def solution(mesh):
    placed = (
        P(("seq", "row"), "col"),
        P(("seq", "row"), "col"),
        P("col", ("seq", "row")),
        P(),
        P(),
        P(),
        P("seq"),
    )
    return jax.shard_map(
        on_device, mesh=mesh, in_specs=placed, out_specs=P(("seq", "row"), "col"), check_vma=False
    )
```

profile of v0, /device:TPU:8, one launch (start us, length us, event | category | flops | bytes accessed | tf_op | source)
XLA Modules:
  0.0 657.6 jit_solution(16882960967085766931)
XLA Ops:
  8.1 30.5 %all-gather.6.cloned.1.call-done = bf16[128,4096]{1,0:T(8,128)(2,1)} async-done(((bf16[128,1024]{1,0:T(8,128)(2,1)}), bf16[128,4096]{1,0:T(8,128)(2,1)}) %all-gather.6.cloned.1.call-update) | async-done | bytes 1048592 | tf_op jit(solution)/shard_map/all_gather | solution.py:30
  38.6 203.7 %all-gather.8.cloned.1.call-done = bf16[4096,2048]{1,0:T(8,128)(2,1)} async-done(((bf16[64,2048]{1,0:T(8,128)(2,1)}), bf16[4096,2048]{1,0:T(8,128)(2,1)}) %all-gather.8.cloned.1.call-update) | async-done | bytes 16777232 | tf_op jit(solution)/shard_map/all_gather | solution.py:38
  242.3 8.5 %multiply_convert_fusion = bf16[128,2048]{1,0:T(8,128)(2,1)S(1)} fusion(bf16[128,4096]{1,0:T(8,128)(2,1)} %all-gather.6.cloned.1.call-done, bf16[4096,2048]{1,0:T(8,128)(2,1)} %all-gather.8.cloned.1.call-done), kind=kOutput, calls=%fused_computation.33 | convolution fusion | flops 2148794368 | bytes 18350080 | tf_op jit(solution)/shard_map/dot_general | solution.py:36
  251.4 27.6 %all_to_all.33 = bf16[128,4,4,128]{3,2,0,1:T(4,128)(2,1)S(1)} all-to-all(bf16[128,4,4,128]{3,2,0,1:T(4,128)(2,1)S(1)} %copy.26), channel_id=1, replica_groups=mesh['seq'=16,'row'=4,'col'=4] {'row'}, dimensions={1} | all-to-all | bytes 1048576 | tf_op jit(solution)/shard_map/all_to_all | solution.py:43
  280.7 14.5 %all-gather = s32[16,1,512]{2,1,0:T(1,128)S(1)} all-gather(s32[1,1,512]{2,1,0:T(1,128)S(1)} %bitcast.80), channel_id=1, replica_groups=mesh['seq'=16,'row'=4,'col'=4] {'seq'}, dimensions={0}, use_global_device_ids=true | all-gather | bytes 34816 | tf_op jit(solution)/shard_map/all_gather | solution.py:57
  296.0 19.7 %all-gather.10.cloned.1.call-done = bf16[8192,1,2,128]{3,0,2,1:T(8,128)(2,1)} async-done(((bf16[512,1,2,128]{3,0,2,1:T(8,128)(2,1)}), bf16[8192,1,2,128]{3,0,2,1:T(8,128)(2,1)}) %all-gather.10.cloned.1.call-update) | async-done | bytes 4194320 | tf_op jit(solution)/shard_map/all_gather | solution.py:56
  315.8 289.0 %while.11 = (s32[]{:T(128)}, f32[512,1,128]{2,0,1:T(8,128)S(1)}, s32[512]{0:T(512)S(1)}, s32[4]{0:T(128)S(1)}, s32[32]{0:T(128)S(1)}, /*index=5*/bf16[8192,1,2,1...) while((s32[]{:T(128)}, f32[512,1,128]{2,0,1:T(8,128)S(1)}, ...), condition=%wide.region_4.5_spmd.clone, body=%wide.region_2.4_spmd.clone.sunk | while | flops 123473408 | bytes 3950976 | solution.py:83
  317.2 5.3 fusion.36
  326.3 5.3 fusion.36
  335.3 5.3 fusion.36
  344.3 5.3 fusion.36
  353.4 5.3 fusion.36
  362.4 5.3 fusion.36
  371.4 5.3 fusion.36
  380.5 5.3 fusion.36
  389.5 5.3 fusion.36
  398.5 5.3 fusion.36
  407.6 5.3 fusion.36
  416.6 5.3 fusion.36
  425.6 5.3 fusion.36
  434.6 5.3 fusion.36
  443.7 5.3 fusion.36
  606.6 15.3 %all_to_all.34 = bf16[4,2,8192]{2,1,0:T(2,128)(2,1)S(1)} all-to-all(bf16[4,2,8192]{2,1,0:T(2,128)(2,1)S(1)} %reshape.130), channel_id=1, replica_groups=mesh['seq'=16,'row'=4,'col'=4] {'row'}, dimensions={0} | all-to-all | bytes 262144 | tf_op jit(solution)/shard_map/all_to_all | solution.py:89
  627.0 22.4 %reduce-scatter.2.cloned.1.call-done = bf16[128,1024]{1,0:T(8,128)(2,1)} async-done(((bf16[128,4096]{1,0:T(8,128)(2,1)}), bf16[128,1024]{1,0:T(8,128)(2,1)}) %reduce-scatter.2.cloned.1.call-update) | async-done | bytes 262160 | tf_op jit(solution)/shard_map/reduce_scatter | solution.py:96
  (317 shorter events, 200.4 us)
Async XLA Ops:
  6.5 289.4 %copy-start = (f32[16,128]{1,0:T(8,128)S(1)}, f32[16,128]{1,0:T(8,128)}, u32[]{:S(2)}) copy-start(f32[16,128]{1,0:T(8,128)} %param.13) | copy-start | bytes 24580
  6.5 32.0 %all-gather.6.cloned.1.call-start = ((), (), s32[]{:S(2)}) async-start(), calls=%async_computation.3 | async-start | bytes 1310720 | tf_op jit(solution)/shard_map/all_gather | solution.py:30
  7.3 235.0 %all-gather.8.cloned.1.call-start = ((), (), s32[]{:S(2)}) async-start(), calls=%async_computation.4 | async-start | bytes 17039360 | tf_op jit(solution)/shard_map/all_gather | solution.py:38
  8.0 307.7 %all-gather.10.cloned.1.call-start = ((), (), s32[]{:S(2)}) async-start(), calls=%async_computation.5 | async-start | bytes 4456448 | tf_op jit(solution)/shard_map/all_gather | solution.py:56
  250.8 29.7 %copy-start.3 = (s32[4]{0:T(128)S(1)}, s32[4]{0:T(128)}, u32[]{:S(2)}) copy-start(s32[4]{0:T(128)} %param.14) | copy-start | bytes 52
  250.8 29.9 %copy-start.2 = (s32[512]{0:T(512)S(1)}, s32[512]{0:T(512)}, u32[]{:S(2)}) copy-start(s32[512]{0:T(512)} %param.15) | copy-start | bytes 6148
  279.9 342.4 %all-gather.12.cloned.1.call-start = ((), (), s32[]{:S(2)}) async-start(), calls=%async_computation.6 | async-start | bytes 4259840 | tf_op jit(solution)/shard_map/all_gather | solution.py:93
  280.5 368.9 %reduce-scatter.2.cloned.1.call-start = ((), (), s32[]{:S(2)}) async-start(), calls=%async_computation.7 | async-start | bytes 1310720 | tf_op jit(solution)/shard_map/reduce_scatter | solution.py:96
  605.4 44.0 %copy-start.1 = (bf16[128,1024]{1,0:T(8,128)(2,1)S(1)}, bf16[128,1024]{1,0:T(8,128)(2,1)}, u32[]{:S(2)}) copy-start(bf16[128,1024]{1,0:T(8,128)(2,1)} %param.9) | copy-start | bytes 786436
Sparse Core Ops, SparseCore 0:
  9.2 29.3 all-gather.5
  40.4 201.8 all-gather.7
  280.0 35.7 all-gather.9
  317.4 185.4 all-gather.11
  627.1 22.2 reduce-scatter.1
where the time goes:
time: 660 us; the launch traced here: 658 us
  waiting for transfers between devices  278 us (42%)
  matrix products  229 us (35%)
  blocking collectives  57.5 us (9%)
  local copies, waits for them, and re-layouts  45.7 us (7%)
  loops' own time  22.8 us (3%)
  between operations  13.3 us (2%)
  other arithmetic  11.2 us (2%)
    all_gather x1, waiting for transfers between devices, on_device(): lax.all_gather(w_uvqk, ('seq', 'row'), axis=0, tiled=True)  204 us
    dot_general x32, matrix products, bucket_biases(): jnp.einsum('qkb,hb->hqk', one_hot, table_rows, precision=lax.Precision.HI...  168 us
    dot_general x32, matrix products, sub_block(): jnp.dot(weights, kv_sub[:, 0, 0], preferred_element_type=jnp.float32)  47.3 us
    all_gather x1, waiting for transfers between devices, on_device(): feature_rows = lax.all_gather(tokens, 'col', axis=1, tiled=True)  30.5 us
    all_to_all x1, blocking collectives, on_device(): lax.all_to_all(activated, 'row', split_axis=1, concat_axis=0, tiled=True)  27.6 us
    another operation x1, loops' own time, on_device(): lax.scan(sub_block, running, jnp.arange(sub_count, dtype=jnp.int32))  22.8 us
    reduce_scatter x1, waiting for transfers between devices, on_device(): lax.psum_scatter(partials.astype(jnp.bfloat16), 'col', scatter_dimension=...  22.4 us
    dot_general x32, local copies, waits for them, and re-layouts, bucket_biases(): jnp.einsum('qkb,hb->hqk', one_hot, table_rows, precision=lax.Precision.HI...  21.5 us
  transfers between devices with their start and end apart: 5, of which 4 were waited for; matrix products, arithmetic and copies ran while one was open for 41% of the time, Pallas kernels for 0%

commit v1 on v0

--- a/solution.py
+++ b/solution.py
@@ -27,7 +27,12 @@
 
 
 def on_device(tokens, w_uvqk, w_out, rab_table, norm_gain, user_lengths, bucket_ids):
-    feature_rows = lax.all_gather(tokens, "col", axis=1, tiled=True)
+    ring = [tokens]
+    for hop in range(3):
+        ring.append(lax.ppermute(ring[-1], "col", [(dev, (dev + 1) % 4) for dev in range(4)]))
+    feature_rows = jnp.roll(
+        jnp.concatenate(ring[::-1], axis=1), (lax.axis_index("col") + 1) * ring[0].shape[1], axis=1
+    )
     local_rows = tokens.shape[0]
     width_cols = w_uvqk.shape[1]
     row_index = lax.axis_index("row")

time: 660 us -> 630 us (0.955)
  waiting for transfers between devices: 278 us -> 246 us
    all_gather x1 -> x0, waiting for transfers between devices: 30.5 us -> none  [on_device(): feature_rows = lax.all_gather(tokens, 'col', axis=1, tiled=True)]
    all_gather x1, waiting for transfers between devices: 204 us -> 180 us  [on_device(): lax.all_gather(w_uvqk, ('seq', 'row'), axis=0, tiled=True)]
    ppermute x0 -> x3, waiting for transfers between devices: none -> 23.7 us  [on_device(): lax.ppermute(ring[-1], 'col', [(dev, (dev + 1) % 4) for dev in range(4)])]
  transfers between devices with their start and end apart: 5 -> 7, of which waited for: 4 -> 6; matrix products, arithmetic and copies ran while one was open for 41% -> 43% of each run, Pallas kernels for 0% -> 0%
where the time goes in v1:
time: 630 us; the launch traced here: 628 us
  waiting for transfers between devices  246 us (39%)
  matrix products  228 us (36%)
  blocking collectives  57.8 us (9%)
  local copies, waits for them, and re-layouts  46.8 us (7%)
  loops' own time  22.8 us (4%)
  between operations  13.3 us (2%)
  other arithmetic  11.2 us (2%)
    all_gather x1, waiting for transfers between devices, on_device(): lax.all_gather(w_uvqk, ('seq', 'row'), axis=0, tiled=True)  180 us
    dot_general x32, matrix products, bucket_biases(): jnp.einsum('qkb,hb->hqk', one_hot, table_rows, precision=lax.Precision.HI...  168 us
    dot_general x32, matrix products, sub_block(): jnp.dot(weights, kv_sub[:, 0, 0], preferred_element_type=jnp.float32)  47.1 us
    all_to_all x1, blocking collectives, on_device(): lax.all_to_all(activated, 'row', split_axis=1, concat_axis=0, tiled=True)  27.6 us
    ppermute x3, waiting for transfers between devices, on_device(): lax.ppermute(ring[-1], 'col', [(dev, (dev + 1) % 4) for dev in range(4)])  23.7 us
    another operation x1, loops' own time, on_device(): lax.scan(sub_block, running, jnp.arange(sub_count, dtype=jnp.int32))  22.8 us
    reduce_scatter x1, waiting for transfers between devices, on_device(): lax.psum_scatter(partials.astype(jnp.bfloat16), 'col', scatter_dimension=...  22 us
    dot_general x32, local copies, waits for them, and re-layouts, bucket_biases(): jnp.einsum('qkb,hb->hqk', one_hot, table_rows, precision=lax.Precision.HI...  21.5 us
  transfers between devices with their start and end apart: 7, of which 6 were waited for; matrix products, arithmetic and copies ran while one was open for 43% of the time, Pallas kernels for 0%

profile of v1, /device:TPU:8, one launch (start us, length us, event | category | flops | bytes accessed | tf_op | source)
XLA Modules:
  0.0 628.2 jit_solution(7569786832721845754)
XLA Ops:
  8.9 8.0 %collective-permute-done = bf16[128,1024]{1,0:T(8,128)(2,1)S(1)} collective-permute-done((bf16[128,1024]{1,0:T(8,128)(2,1)}, bf16[128,1024]{1,0:T(8,128)(2,1)S(1)}, u32[]{:S(2)}, u32[]{:S(2)}) %collective-permute-start) | collective-permute-done | bytes 262176 | tf_op jit(solution)/shard_map/ppermute | solution.py:32
  17.1 8.1 %collective-permute-done.1 = bf16[128,1024]{1,0:T(8,128)(2,1)S(1)} collective-permute-done((bf16[128,1024]{1,0:T(8,128)(2,1)S(1)}, bf16[128,1024]{1,0:T(8,128)(2,1)S(1)}, u32[]{:S(2)}, u32[]{:S(2)}) %collective-permute-start.1) | collective-permute-done | bytes 262176 | tf_op jit(solution)/shard_map/ppermute | solution.py:32
  25.2 7.6 %collective-permute-done.2 = bf16[128,1024]{1,0:T(8,128)(2,1)S(1)} collective-permute-done((bf16[128,1024]{1,0:T(8,128)(2,1)S(1)}, bf16[128,1024]{1,0:T(8,128)(2,1)S(1)}, u32[]{:S(2)}, u32[]{:S(2)}) %collective-permute-start.2) | collective-permute-done | bytes 262176 | tf_op jit(solution)/shard_map/ppermute | solution.py:32
  34.0 179.6 %all-gather.5.cloned.1.call-done = bf16[4096,2048]{1,0:T(8,128)(2,1)} async-done(((bf16[64,2048]{1,0:T(8,128)(2,1)}), bf16[4096,2048]{1,0:T(8,128)(2,1)}) %all-gather.5.cloned.1.call-update) | async-done | bytes 16777232 | tf_op jit(solution)/shard_map/all_gather | solution.py:43
  213.6 8.2 %multiply_convert_fusion = bf16[128,2048]{1,0:T(8,128)(2,1)S(1)} fusion(bf16[4096,2048]{1,0:T(8,128)(2,1)} %all-gather.5.cloned.1.call-done, bf16[128,8192]{1,0:T(8,128)(2,1)S(1)} %constant_dynamic-update-slice_fusion, s32[]{:T(128)S(6)} %select_n.26), kind=kOutput, calls=%fused_computation.33 | convolution fusion | flops 2148794368 | bytes 18350084 | tf_op jit(solution)/shard_map/dot_general | solution.py:41
  222.4 27.6 %all_to_all.33 = bf16[128,4,4,128]{3,2,0,1:T(4,128)(2,1)S(1)} all-to-all(bf16[128,4,4,128]{3,2,0,1:T(4,128)(2,1)S(1)} %copy.26), channel_id=1, replica_groups=mesh['seq'=16,'row'=4,'col'=4] {'row'}, dimensions={1} | all-to-all | bytes 1048576 | tf_op jit(solution)/shard_map/all_to_all | solution.py:48
  251.9 14.8 %all-gather = s32[16,1,512]{2,1,0:T(1,128)S(1)} all-gather(s32[1,1,512]{2,1,0:T(1,128)S(1)} %bitcast.79), channel_id=1, replica_groups=mesh['seq'=16,'row'=4,'col'=4] {'seq'}, dimensions={0}, use_global_device_ids=true | all-gather | bytes 34816 | tf_op jit(solution)/shard_map/all_gather | solution.py:62
  267.4 19.3 %all-gather.7.cloned.1.call-done = bf16[8192,1,2,128]{3,0,2,1:T(8,128)(2,1)} async-done(((bf16[512,1,2,128]{3,0,2,1:T(8,128)(2,1)}), bf16[8192,1,2,128]{3,0,2,1:T(8,128)(2,1)}) %all-gather.7.cloned.1.call-update) | async-done | bytes 4194320 | tf_op jit(solution)/shard_map/all_gather | solution.py:61
  286.7 288.9 %while.11 = (s32[]{:T(128)}, f32[512,1,128]{2,0,1:T(8,128)S(1)}, s32[512]{0:T(512)S(1)}, s32[4]{0:T(128)S(1)}, s32[32]{0:T(128)S(1)}, /*index=5*/bf16[8192,1,2,1...) while((s32[]{:T(128)}, f32[512,1,128]{2,0,1:T(8,128)S(1)}, ...), condition=%wide.region_4.5_spmd.clone, body=%wide.region_2.4_spmd.clone.sunk | while | flops 123473408 | bytes 3950976 | solution.py:88
  288.2 5.3 fusion.41
  297.3 5.3 fusion.41
  306.3 5.3 fusion.41
  315.3 5.3 fusion.41
  324.3 5.3 fusion.41
  333.4 5.3 fusion.41
  342.4 5.3 fusion.41
  351.4 5.3 fusion.41
  360.5 5.3 fusion.41
  369.5 5.3 fusion.41
  405.6 5.3 fusion.41
  450.7 5.3 fusion.41
  541.0 5.3 fusion.41
  577.5 15.4 %all_to_all.34 = bf16[4,2,8192]{2,1,0:T(2,128)(2,1)S(1)} all-to-all(bf16[4,2,8192]{2,1,0:T(2,128)(2,1)S(1)} %reshape.130), channel_id=1, replica_groups=mesh['seq'=16,'row'=4,'col'=4] {'row'}, dimensions={0} | all-to-all | bytes 262144 | tf_op jit(solution)/shard_map/all_to_all | solution.py:94
  597.9 22.0 %reduce-scatter.2.cloned.1.call-done = bf16[128,1024]{1,0:T(8,128)(2,1)} async-done(((bf16[128,4096]{1,0:T(8,128)(2,1)}), bf16[128,1024]{1,0:T(8,128)(2,1)}) %reduce-scatter.2.cloned.1.call-update) | async-done | bytes 262160 | tf_op jit(solution)/shard_map/reduce_scatter | solution.py:101
  (328 shorter events, 213.1 us)
Async XLA Ops:
  6.5 260.8 %copy-start = (f32[16,128]{1,0:T(8,128)S(1)}, f32[16,128]{1,0:T(8,128)}, u32[]{:S(2)}) copy-start(f32[16,128]{1,0:T(8,128)} %param.13) | copy-start | bytes 24580
  6.5 27.4 %copy-start.1 = (bf16[128,1024]{1,0:T(8,128)(2,1)S(1)}, bf16[128,1024]{1,0:T(8,128)(2,1)}, u32[]{:S(2)}) copy-start(bf16[128,1024]{1,0:T(8,128)(2,1)} %param.9) | copy-start | bytes 786436
  6.5 207.0 %all-gather.5.cloned.1.call-start = ((), (), s32[]{:S(2)}) async-start(), calls=%async_computation.3 | async-start | bytes 17039360 | tf_op jit(solution)/shard_map/all_gather | solution.py:43
  7.3 279.5 %all-gather.7.cloned.1.call-start = ((), (), s32[]{:S(2)}) async-start(), calls=%async_computation.4 | async-start | bytes 4456448 | tf_op jit(solution)/shard_map/all_gather | solution.py:61
  7.3 9.5 %collective-permute-start = (bf16[128,1024]{1,0:T(8,128)(2,1)}, bf16[128,1024]{1,0:T(8,128)(2,1)S(1)}, u32[]{:S(2)}, u32[]{:S(2)}) collective-permute-start(bf16[128,1024]{1,0:T(8,128)(2,1)} %param.9), channel_id=1, source_target_pairs={{0,1},{1,2},{2,3},{3,0},{4,5},{5,6},{6,7},{7,4},{8,9},{9,10},{10,1... | collective-permute-start | bytes 786440 | tf_op jit(solution)/shard_map/ppermute | solution.py:32
  16.9 8.4 %collective-permute-start.1 = (bf16[128,1024]{1,0:T(8,128)(2,1)S(1)}, bf16[128,1024]{1,0:T(8,128)(2,1)S(1)}, u32[]{:S(2)}, u32[]{:S(2)}) collective-permute-start(bf16[128,1024]{1,0:T(8,128)(2,1)S(1)} %collective-permute-done), channel_id=1, source_target_pairs={{0,1},{1,2},{2,3},{3,0},{4,5},{5,6},{6,7},{7,4},{8,9},{9,10},{10,1... | collective-permute-start | bytes 786440 | tf_op jit(solution)/shard_map/ppermute | solution.py:32
  25.2 7.6 %collective-permute-start.2 = (bf16[128,1024]{1,0:T(8,128)(2,1)S(1)}, bf16[128,1024]{1,0:T(8,128)(2,1)S(1)}, u32[]{:S(2)}, u32[]{:S(2)}) collective-permute-start(bf16[128,1024]{1,0:T(8,128)(2,1)S(1)} %collective-permute-done.1), channel_id=1, source_target_pairs={{0,1},{1,2},{2,3},{3,0},{4,5},{5,6},{6,7},{7,4},{8,9},{9,10},{10,1... | collective-permute-start | bytes 786440 | tf_op jit(solution)/shard_map/ppermute | solution.py:32
  222.1 29.5 %copy-start.3 = (s32[4]{0:T(128)S(1)}, s32[4]{0:T(128)}, u32[]{:S(2)}) copy-start(s32[4]{0:T(128)} %param.14) | copy-start | bytes 52
  222.2 29.7 %copy-start.2 = (s32[512]{0:T(512)S(1)}, s32[512]{0:T(512)}, u32[]{:S(2)}) copy-start(s32[512]{0:T(512)} %param.15) | copy-start | bytes 6148
  250.9 342.4 %all-gather.9.cloned.1.call-start = ((), (), s32[]{:S(2)}) async-start(), calls=%async_computation.5 | async-start | bytes 4259840 | tf_op jit(solution)/shard_map/all_gather | solution.py:98
  251.6 368.3 %reduce-scatter.2.cloned.1.call-start = ((), (), s32[]{:S(2)}) async-start(), calls=%async_computation.6 | async-start | bytes 1310720 | tf_op jit(solution)/shard_map/reduce_scatter | solution.py:101
Sparse Core Ops, SparseCore 0:
  9.2 204.3 all-gather.4
  251.0 35.7 all-gather.6
  288.6 185.4 all-gather.8
  598.0 21.8 reduce-scatter.1
